TPU v7x, 32 devices: a whole 2x2x4 slice. The times are simulated.
32 devices in a mesh: gx: 8 (over z, y), gy: 4 (over x, core).
Axes of the slice: x: 2, y: 2, z: 4, core: 2. Of those that a mesh axis runs over, the one named last changes fastest.
Arguments:
- layer_input: bfloat16 [128, 128, 32, 512], P('gx', 'gy'), may hold values from -6 to 6
- cotangent: bfloat16 [128, 128, 32, 512], P('gx', 'gy'), may hold values from -6 to 6
- spectral_weight: bfloat16 [32, 64, 32, 1024], P('gy', 'gx'), may hold values from -12 to 12
- bypass_weight: bfloat16 [32, 32], replicated, may hold values from -1 to 1
- channel_bias: float32 [32], replicated, may hold values from -4 to 4
- hash_key: int32 [2], replicated, may hold values from 0 to 1073741823
Outputs:
- grad_input: bfloat16 [128, 128, 32, 512], P('gx', 'gy')
- grad_spectral: float32 [32, 64, 32, 1024], P('gy', 'gx')
- grad_bypass: float32 [32, 32], replicated
- grad_bias: float32 [32], replicated
All inputs are finite; a program needn't handle non-finite values.
Results may differ from a plain program's by a relative error of at most 0.011.
Values sent between devices are 32-bit elements; how exact they have to be, the bound alone decides.
A program may use at most 192 MiB of HBM per device.

v0:
```python
import math

import jax
import jax.numpy as jnp
from jax import lax
from jax.sharding import PartitionSpec as P

LX = 128
LY = 128
LZ = 64
LT = 8
KX = 32
KY = 32
KZ = 16
KT = 4
LZT = 512


keep_level = 6554
keep_scale = 1.0 / 0.9
gelu_cubic = 0.044715
mixer_one = -1640531535
mixer_two = -2048144789
mixer_three = -1028477387


def hartley_table(kept, length):
    wanted = jnp.arange(kept, dtype=jnp.int32)
    frequency = jnp.where(wanted < kept // 2, wanted, wanted + (length - kept))
    positions = jnp.arange(length, dtype=jnp.int32)
    residue = frequency[:, None] * positions[None, :] % length
    radians = residue.astype(jnp.float32) * (2.0 * math.pi / length)
    return (jnp.cos(radians) + jnp.sin(radians)) / math.sqrt(length)


def depth_table():
    depth_part = hartley_table(KZ, LZ)
    time_part = hartley_table(KT, LT)
    joined = depth_part[:, None, :, None] * time_part[None, :, None, :]
    return joined.reshape(KZ * KT, LZ * LT)


def scramble(hashed):
    hashed = jnp.bitwise_xor(hashed, lax.shift_right_logical(hashed, jnp.int32(16)))
    hashed = hashed * jnp.int32(mixer_two)
    hashed = jnp.bitwise_xor(hashed, lax.shift_right_logical(hashed, jnp.int32(13)))
    hashed = hashed * jnp.int32(mixer_three)
    return jnp.bitwise_xor(hashed, lax.shift_right_logical(hashed, jnp.int32(16)))


def dropout_keep(cell_index, hash_key):
    hashed = cell_index * jnp.int32(mixer_one) + hash_key[0]
    hashed = scramble(hashed)
    hashed = scramble(jnp.bitwise_xor(hashed, hash_key[1]))
    return jnp.bitwise_and(hashed, jnp.int32(65535)) >= keep_level


def gelu_slope(preact):
    factor = math.sqrt(2.0 / math.pi)
    tanh_value = jnp.tanh(factor * (preact + gelu_cubic * preact * preact * preact))
    return 0.5 * (1.0 + tanh_value) + 0.5 * preact * (1.0 - tanh_value * tanh_value) * factor * (
        1.0 + 3.0 * gelu_cubic * preact * preact
    )


def local(layer_input, cotangent, spectral_weight, bypass_weight, channel_bias, hash_key):
    highest = lax.Precision.HIGHEST
    slab_rows, slab_columns, channels, depth_cells = layer_input.shape
    column_devices = lax.axis_size("gy")
    row_offset = lax.axis_index("gx") * slab_rows
    column_offset = lax.axis_index("gy") * slab_columns
    across_table = hartley_table(KX, LX)
    down_table = lax.dynamic_slice_in_dim(hartley_table(KY, LY), column_offset, slab_columns, 1)
    depth_full = depth_table()
    depth_low = depth_full.T.astype(jnp.bfloat16)
    weight_modes = spectral_weight.astype(jnp.float32).reshape(
        spectral_weight.shape[0],
        spectral_weight.shape[1],
        spectral_weight.shape[2],
        channels,
        channels,
    )

    def forward_modes(source):
        depth_flat = jnp.dot(
            source.reshape(-1, depth_cells), depth_low, preferred_element_type=jnp.float32
        )
        partial_depth = depth_flat.reshape(slab_rows, slab_columns, channels, depth_low.shape[1])
        at_owner = lax.all_to_all(partial_depth, "gx", split_axis=3, concat_axis=0, tiled=True)
        swept = jnp.einsum("jx,xycm->jycm", across_table, at_owner, precision=highest)
        return lax.psum_scatter(
            jnp.einsum("ky,jycm->kmjc", down_table, swept, precision=highest),
            "gy",
            scatter_dimension=0,
            tiled=True,
        )

    def inverse_modes(mode_block):
        gathered = jnp.einsum(
            "ky,kmjc->jycm",
            down_table,
            lax.all_gather(mode_block, "gy", axis=0, tiled=True),
            precision=highest,
        )
        planes = jnp.einsum("jx,jycm->xycm", across_table, gathered, precision=highest)
        cell_modes = lax.all_to_all(planes, "gx", split_axis=0, concat_axis=3, tiled=True)
        flattened = jnp.dot(
            cell_modes.reshape(-1, cell_modes.shape[3]),
            depth_full,
            precision=highest,
            preferred_element_type=jnp.float32,
        )
        return flattened.reshape(slab_rows, slab_columns, channels, depth_cells)

    input_modes = forward_modes(layer_input)
    bypass = jnp.einsum(
        "xyct,cd->xydt", layer_input, bypass_weight, preferred_element_type=jnp.float32
    )
    row_ids = row_offset + jnp.arange(slab_rows, dtype=jnp.int32)
    column_ids = column_offset + jnp.arange(slab_columns, dtype=jnp.int32)
    channel_ids = jnp.arange(channels, dtype=jnp.int32)
    depth_ids = jnp.arange(depth_cells, dtype=jnp.int32)
    all_columns = slab_columns * column_devices
    cell_index = (
        (row_ids[:, None, None, None] * all_columns + column_ids[None, :, None, None]) * channels
        + channel_ids[None, None, :, None]
    ) * depth_cells + depth_ids[None, None, None, :]
    keep_mask = dropout_keep(cell_index, hash_key)
    mixed_modes = jnp.einsum("kmjc,kmjcd->kmjd", input_modes, weight_modes, precision=highest)
    spectral = inverse_modes(mixed_modes)
    preact = spectral + bypass + channel_bias[None, None, :, None]
    dpre = jnp.where(
        keep_mask, cotangent.astype(jnp.float32) * gelu_slope(preact) * keep_scale, 0.0
    ).astype(jnp.bfloat16)
    weight_local = jnp.einsum(
        "xyct,xydt->cd", layer_input, dpre, preferred_element_type=jnp.float32
    )
    bias_local = jnp.sum(dpre.astype(jnp.float32), axis=(0, 1, 3))
    weight_total, bias_total = lax.psum((weight_local, bias_local), ("gx", "gy"))
    norm_scale = 1.0 / math.sqrt(LX * LY * LZT)
    dpre_modes = forward_modes(dpre)
    grad_spectral = (input_modes[:, :, :, :, None] * dpre_modes[:, :, :, None, :]).reshape(
        spectral_weight.shape
    )
    backward_modes = jnp.einsum("kmjd,kmjcd->kmjc", dpre_modes, weight_modes, precision=highest)
    local_back = jnp.einsum(
        "xydt,cd->xyct", dpre, bypass_weight, preferred_element_type=jnp.float32
    )
    grad_input = (inverse_modes(backward_modes) + local_back).astype(jnp.bfloat16)
    return (grad_input, grad_spectral, weight_total * norm_scale, bias_total * norm_scale)


def solution(mesh):
    return jax.shard_map(
        local,
        mesh=mesh,
        in_specs=(
            P("gx", "gy", None, None),
            P("gx", "gy", None, None),
            P("gy", "gx", None, None),
            P(),
            P(),
            P(),
        ),
        out_specs=(P("gx", "gy", None, None), P("gy", "gx", None, None), P(), P()),
        check_vma=False,
    )
```

profile of v0, /device:TPU:13, one launch (start us, length us, event | category | flops | bytes accessed | tf_op | source)
XLA Modules:
  0.0 1237.1 jit_solution(3583566027194761349)
XLA Ops:
  7.9 1.5 convert_element_type.67
  9.4 12.9 %convolution_bitcast_fusion = f32[16384,64]{0,1:T(8,128)} fusion(bf16[64,512]{1,0:T(8,128)(2,1)S(1)} %convert_element_type.67, bf16[16384,512]{1,0:T(8,128)(2,1)} %bitcast.137), kind=kOutput, calls=%fused_computation.29 | convolution fusion | flops 1073741824 | bytes 21037056 | tf_op jit(solution)/shard_map/dot_general | solution.py:85
  22.4 6.9 copy.51
  29.2 16.2 %copy.52 = f32[16,32,32,64]{2,1,0,3:T(8,128)} copy(f32[16,32,32,64]{3,2,1,0:T(8,128)} %bitcast.146) | data formatting | bytes 8388608 | tf_op jit(solution)/shard_map/reshape | solution.py:88
  45.4 12.8 %reshape.222 = f32[8,1,131072]{2,1,0:T(1,128)} reshape(f32[64,16,32,32]{3,2,1,0:T(8,128)} %bitcast.138) | data formatting | bytes 8388608
  58.3 5.7 all-to-all-start
  64.3 90.3 %all-to-all-done = f32[8,1,131072]{2,1,0:T(1,128)} async-done(((f32[8,1,131072]{2,1,0:T(1,128)}), f32[8,1,131072]{2,1,0:T(1,128)}, u32[]{:S(2)}, u32[]{:S(2)}) %all-to-all-start) | async-done | bytes 4194336 | tf_op jit(solution)/shard_map/all_to_all | solution.py:89
  154.6 0.5 broadcast.314
  155.1 14.6 %reduce = f32[8,131072]{1,0:T(8,128)} reduce(f32[8,1,131072]{2,1,0:T(1,128)} %all-to-all-done, f32[]{:T(128)} %broadcast.314), dimensions={1}, to_apply=%all_to_all.48.reduce_sub_computation | reduce | bytes 8388612 | tf_op jit(solution)/shard_map/all_to_all | solution.py:89
  169.7 13.8 %reshape.223 = f32[64,16,32,32]{3,2,1,0:T(8,128)} reshape(f32[8,131072]{1,0:T(8,128)} %reduce) | data formatting | bytes 8388608
  183.5 19.4 %copy.54 = f32[8,16,32,32,8]{3,4,2,1,0:T(8,128)S(1)} copy(f32[8,16,32,32,8]{3,2,1,4,0:T(8,128)} %bitcast.142) | data formatting | bytes 8388608 | tf_op jit(solution)/shard_map/all_to_all | solution.py:89
  202.9 18.9 %fusion.26 = f32[32,32,32,8]{2,0,3,1:T(8,128)S(1)} fusion(f32[128,32,32,8]{2,3,1,0:T(8,128)S(1)} %bitcast.144, s32[32]{0:T(128)S(1)} %compare_select_fusion.2), kind=kOutput, calls=%fused_computation.38 | convolution fusion | flops 402718720 | bytes 5243008 | tf_op jit(solution)/shard_map/jx,xycm->jycm/dot_general | solution.py:90
  221.8 11.5 fusion.32
  233.3 6.4 copy.57
  239.7 20.8 %reshape.208 = bf16[8,8,32,32,32]{4,3,2,1,0:T(8,128)(2,1)} reshape(bf16[8,8,32,1024]{3,2,1,0:T(8,128)(2,1)} %param.8) | data formatting | bytes 8388608 | tf_op jit(solution)/shard_map/reshape | solution.py:76
  260.5 25.6 %reduce-scatter.3.cloned.1.call-done = f32[8,8,32,32]{3,2,1,0:T(8,128)} async-done(((f32[32,8,32,32]{3,2,1,0:T(8,128)}), f32[8,8,32,32]{3,2,1,0:T(8,128)}) %reduce-scatter.3.cloned.1.call-update) | async-done | bytes 262160 | tf_op jit(solution)/shard_map/reduce_scatter | solution.py:91
  286.0 15.8 %fusion.99 = f32[8,8,32,1,32]{4,3,2,1,0:T(1,128)S(1)} fusion(f32[8,8,32,32,1]{3,4,2,1,0:T(1,128)} %bitcast.149, bf16[8,8,32,32,32]{4,3,2,1,0:T(8,128)(2,1)} %reshape.208), kind=kOutput, calls=%fused_computation.135 | convolution fusion | flops 25165824 | bytes 4718592 | tf_op jit(solution)/shard_map/kmjc,kmjcd->kmjd/dot_general | solution.py:129
  301.8 1.6 copy.113
  303.4 35.6 %all-gather.3.cloned.1.call-done = f32[32,8,32,32]{3,0,2,1:T(8,128)} async-done(((f32[8,8,32,32]{3,0,2,1:T(8,128)}), f32[32,8,32,32]{3,0,2,1:T(8,128)}) %all-gather.3.cloned.1.call-update) | async-done | bytes 1048592 | tf_op jit(solution)/shard_map/all_gather | solution.py:102
  339.0 9.8 convolution_bitcast_fusion.2
  348.8 6.9 copy.58
  355.8 6.8 fusion.53
  362.6 14.5 %copy.59 = f32[128,32,32,8]{2,3,1,0:T(8,128)} copy(f32[128,32,32,8]{0,2,3,1:T(8,128)} %fusion.53) | data formatting | bytes 8388608 | tf_op jit(solution)/shard_map/jx,jycm->xycm/dot_general | solution.py:105
  377.1 12.8 %reshape.224 = f32[8,1,131072]{2,1,0:T(1,128)} reshape(f32[128,32,8,32]{3,2,1,0:T(8,128)} %bitcast.139) | data formatting | bytes 8388608
  389.9 5.5 all-to-all-start.1
  395.4 1.5 reshape.215
  396.9 1.2 reshape.213
  398.1 0.5 fusion.98
  398.9 87.1 %all-to-all-done.1 = f32[8,1,131072]{2,1,0:T(1,128)} async-done(((f32[8,1,131072]{2,1,0:T(1,128)}), f32[8,1,131072]{2,1,0:T(1,128)}, u32[]{:S(2)}, u32[]{:S(2)}) %all-to-all-start.1) | async-done | bytes 4194336 | tf_op jit(solution)/shard_map/all_to_all | solution.py:106
  486.0 14.6 %reduce.1 = f32[8,131072]{1,0:T(8,128)} reduce(f32[8,1,131072]{2,1,0:T(1,128)} %all-to-all-done.1, f32[]{:T(128)} %broadcast.314), dimensions={1}, to_apply=%all_to_all.52.reduce_sub_computation | reduce | bytes 8388612 | tf_op jit(solution)/shard_map/all_to_all | solution.py:106
  500.7 13.3 %reshape.225 = f32[128,32,8,32]{3,2,1,0:T(8,128)} reshape(f32[8,131072]{1,0:T(8,128)} %reduce.1) | data formatting | bytes 8388608
  514.0 32.7 %fusion.20 = f32[16,32,32,512]{3,2,1,0:T(8,128)} fusion(f32[16,32,32,8,8]{2,4,1,0,3:T(8,128)} %bitcast.136, f32[64,512,1,1]{1,0,2,3:T(8,128)S(1)} %reshape.213), kind=kOutput, calls=%fused_computation.32 | convolution fusion | flops 6442450944 | bytes 37879808 | tf_op jit(solution)/shard_map/dot_general | solution.py:107
  546.8 59.6 %convert_reduce_fusion = (f32[32]{0:T(128)S(1)}, bf16[16,32,32,512]{3,2,1,0:T(8,128)(2,1)S(1)}) fusion(f32[32]{0:T(128)S(1)} %copy-done.11, f32[16,32,32,512]{3,2,1,0:T(8,128)} %fusion.20, bf16[16,32,32,512]{3,2,1,0:T(8,128)(2,1)} %param.6, bf16[32,32]{1,0:T(8,128)(2,1)S(1)} %copy-done, bf16[16,32,32,512]{3,2,1,0:T(8,128)(2,1)} %param.7, s32[]{:T(128)} %bitcast.4, ...), kind=kOutput, calls=%fused_computation.27 | convolution fusion | flops 939524096 | bytes 83953928 | tf_op jit(solution)/shard_map/xyct,cd->xydt/dot_general | solution.py:116
  606.4 5.7 copy-done.1
  612.1 6.7 fusion.41
  618.7 16.2 %copy.63 = f32[16,32,32,64]{2,1,0,3:T(8,128)} copy(f32[16,32,32,64]{3,2,1,0:T(8,128)} %fusion.41) | data formatting | bytes 8388608 | tf_op jit(solution)/shard_map/dot_general | solution.py:85
  635.0 12.8 %reshape.226 = f32[8,1,131072]{2,1,0:T(1,128)} reshape(f32[64,16,32,32]{3,2,1,0:T(8,128)} %bitcast.140) | data formatting | bytes 8388608
  647.8 96.7 %all_to_all.66 = f32[8,1,131072]{2,1,0:T(1,128)} all-to-all(f32[8,1,131072]{2,1,0:T(1,128)} %reshape.226), channel_id=1, replica_groups=mesh['gx'=8,'gy'=4] {'gx'}, dimensions={0} | all-to-all | bytes 8388608 | tf_op jit(solution)/shard_map/all_to_all | solution.py:89
  744.5 14.6 %reduce.2 = f32[8,131072]{1,0:T(8,128)} reduce(f32[8,1,131072]{2,1,0:T(1,128)} %all_to_all.66, f32[]{:T(128)} %broadcast.314), dimensions={1}, to_apply=%all_to_all.55.reduce_sub_computation | reduce | bytes 8388612 | tf_op jit(solution)/shard_map/all_to_all | solution.py:89
  759.1 13.4 %reshape.227 = f32[64,16,32,32]{3,2,1,0:T(8,128)} reshape(f32[8,131072]{1,0:T(8,128)} %reduce.2) | data formatting | bytes 8388608
  772.5 19.4 %copy.65 = f32[8,16,32,32,8]{3,4,2,1,0:T(8,128)S(1)} copy(f32[8,16,32,32,8]{3,2,1,4,0:T(8,128)} %bitcast.143) | data formatting | bytes 8388608 | tf_op jit(solution)/shard_map/all_to_all | solution.py:89
  791.9 18.9 %fusion.23 = f32[32,32,32,8]{2,0,3,1:T(8,128)S(1)} fusion(f32[128,32,32,8]{2,3,1,0:T(8,128)S(1)} %bitcast.145, s32[32]{0:T(128)S(1)} %copy-done.9), kind=kOutput, calls=%fused_computation.35 | convolution fusion | flops 402718720 | bytes 5243008 | tf_op jit(solution)/shard_map/jx,xycm->jycm/dot_general | solution.py:90
  810.8 11.5 fusion.35
  822.3 6.4 copy.68
  828.7 46.1 %reduce-scatter.5.cloned.1.call-done = f32[8,8,32,32]{3,2,1,0:T(8,128)} async-done(((f32[32,8,32,32]{3,2,1,0:T(8,128)}), f32[8,8,32,32]{3,2,1,0:T(8,128)}) %reduce-scatter.5.cloned.1.call-update) | async-done | bytes 262160 | tf_op jit(solution)/shard_map/reduce_scatter | solution.py:91
  874.9 29.0 %fusion.100 = f32[8,8,32,1,32]{4,3,2,1,0:T(1,128)S(1)} fusion(f32[8,8,32,32,1]{3,4,2,1,0:T(1,128)} %bitcast.150, bf16[8,8,32,32,32]{4,3,2,1,0:T(8,128)(2,1)} %reshape.208), kind=kOutput, calls=%fused_computation.136 | convolution fusion | flops 25165824 | bytes 4718592 | tf_op jit(solution)/shard_map/kmjd,kmjcd->kmjc/dot_general | solution.py:145
  903.9 1.6 copy.112
  905.5 35.6 %all-gather.5.cloned.1.call-done = f32[32,8,32,32]{3,0,2,1:T(8,128)} async-done(((f32[8,8,32,32]{3,0,2,1:T(8,128)}), f32[32,8,32,32]{3,0,2,1:T(8,128)}) %all-gather.5.cloned.1.call-update) | async-done | bytes 1048592 | tf_op jit(solution)/shard_map/all_gather | solution.py:102
  941.1 9.8 convolution_bitcast_fusion.1
  950.9 6.9 copy.69
  957.8 6.8 fusion.50
  964.6 14.5 %copy.70 = f32[128,32,32,8]{2,3,1,0:T(8,128)} copy(f32[128,32,32,8]{0,2,3,1:T(8,128)} %fusion.50) | data formatting | bytes 8388608 | tf_op jit(solution)/shard_map/jx,jycm->xycm/dot_general | solution.py:105
  979.1 12.8 %reshape.228 = f32[8,1,131072]{2,1,0:T(1,128)} reshape(f32[128,32,8,32]{3,2,1,0:T(8,128)} %bitcast.141) | data formatting | bytes 8388608
  991.9 5.5 all-to-all-start.3
  997.4 13.0 %convolution_bitcast_fusion.3 = f32[32,32]{0,1:T(8,128)S(1)} fusion(bf16[16,32,32,512]{3,2,1,0:T(8,128)(2,1)} %copy-done.1, bf16[16,32,32,512]{3,2,1,0:T(8,128)(2,1)} %param.6), kind=kOutput, calls=%fused_computation.49 | convolution fusion | flops 536870912 | bytes 33558528 | tf_op jit(solution)/shard_map/xyct,xydt->cd/dot_general | solution.py:135
  1010.4 98.1 %all-reduce = (f32[32,32]{0,1:T(8,128)S(1)}, f32[32]{0:T(128)S(1)}) all-reduce(f32[32,32]{0,1:T(8,128)S(1)} %convolution_bitcast_fusion.3, f32[32]{0:T(128)S(1)} %get-tuple-element.26), channel_id=1, replica_groups=mesh['gx'=8,'gy'=4] {'gx','gy'}, use_global_device_ids=true, to_apply=%region_2.3 | all-reduce | flops 1056 | bytes 8448 | tf_op jit(solution)/shard_map/psum | solution.py:139
  1108.5 0.7 copy.73
  1109.2 0.5 broadcast_multiply_fusion.3
  1109.7 11.5 broadcast_multiply_fusion
  1121.2 26.1 %mul.391 = f32[8,8,32,1024]{3,2,1,0:T(8,128)} reshape(f32[8,8,32,32,32]{4,3,2,1,0:T(8,128)} %broadcast_multiply_fusion) | data formatting | bytes 16777216 | tf_op jit(solution)/shard_map/mul | solution.py:142
  1147.2 14.6 %reduce.3 = f32[8,131072]{1,0:T(8,128)} reduce(f32[8,1,131072]{2,1,0:T(1,128)} %all-to-all-done.3, f32[]{:T(128)} %broadcast.314), dimensions={1}, to_apply=%all_to_all.59.reduce_sub_computation | reduce | bytes 8388612 | tf_op jit(solution)/shard_map/all_to_all | solution.py:106
  1161.8 13.8 %reshape.229 = f32[128,32,8,32]{3,2,1,0:T(8,128)} reshape(f32[8,131072]{1,0:T(8,128)} %reduce.3) | data formatting | bytes 8388608
  1175.6 32.6 %fusion.18 = f32[16,32,32,512]{3,2,1,0:T(8,128)} fusion(f32[16,32,32,8,8]{2,4,1,0,3:T(8,128)} %bitcast.135, f32[64,512,1,1]{1,0,2,3:T(8,128)S(1)} %copy-done.3), kind=kOutput, calls=%fused_computation.30 | convolution fusion | flops 6442450944 | bytes 37879808 | tf_op jit(solution)/shard_map/dot_general | solution.py:107
  1208.2 22.2 %fusion.15 = bf16[16,32,32,512]{3,2,1,0:T(8,128)(2,1)} fusion(f32[16,32,32,512]{3,2,1,0:T(8,128)} %fusion.18, bf16[16,32,32,512]{3,2,1,0:T(8,128)(2,1)} %copy-done.1, bf16[32,32]{1,0:T(8,128)(2,1)S(1)} %copy-done), kind=kOutput, calls=%fused_computation.24 | convolution fusion | flops 553648128 | bytes 67110912 | tf_op jit(solution)/shard_map/xydt,cd->xyct/dot_general | solution.py:146
  (44 shorter events, 1.5 us)
Async XLA Ops:
  7.2 539.6 %copy-start = (bf16[32,32]{1,0:T(8,128)(2,1)S(1)}, bf16[32,32]{1,0:T(8,128)(2,1)}, u32[]{:S(2)}) copy-start(bf16[32,32]{1,0:T(8,128)(2,1)} %param.9) | copy-start | bytes 6148
  58.3 96.3 %all-to-all-start = ((f32[8,1,131072]{2,1,0:T(1,128)}), f32[8,1,131072]{2,1,0:T(1,128)}, u32[]{:S(2)}, u32[]{:S(2)}) async-start(f32[8,1,131072]{2,1,0:T(1,128)} %reshape.222), calls=%async_computation | async-start | bytes 8388608 | tf_op jit(solution)/shard_map/all_to_all | solution.py:89
  63.9 222.1 %reduce-scatter.3.cloned.1.call-start = ((), (), s32[]{:S(2)}) async-start(), calls=%async_computation.6 | async-start | bytes 5242880 | tf_op jit(solution)/shard_map/reduce_scatter | solution.py:91
  64.1 291.6 %copy-start.8 = (s32[32]{0:T(128)}, s32[32]{0:T(128)S(1)}, u32[]{:S(2)}) copy-start(s32[32]{0:T(128)S(1)} %compare_select_fusion.2) | copy-start | bytes 388
  64.3 274.7 %copy-start.6 = (f32[32,128]{1,0:T(8,128)}, f32[32,128]{1,0:T(8,128)S(1)}, u32[]{:S(2)}) copy-start(f32[32,128]{1,0:T(8,128)S(1)} %add_multiply_fusion.1) | copy-start | bytes 49156
  239.7 99.3 %all-gather.3.cloned.1.call-start = ((), (), s32[]{:S(2)}) async-start(), calls=%async_computation.7 | async-start | bytes 5242880 | tf_op jit(solution)/shard_map/all_gather | solution.py:102
  377.1 21.0 %copy-start.10 = (s32[2]{0:T(128)S(1)}, s32[2]{0:T(128)}, u32[]{:S(2)}) copy-start(s32[2]{0:T(128)} %param.11) | copy-start | bytes 28
  389.9 96.1 %all-to-all-start.1 = ((f32[8,1,131072]{2,1,0:T(1,128)}), f32[8,1,131072]{2,1,0:T(1,128)}, u32[]{:S(2)}, u32[]{:S(2)}) async-start(f32[8,1,131072]{2,1,0:T(1,128)} %reshape.224), calls=%async_computation.2 | async-start | bytes 8388608 | tf_op jit(solution)/shard_map/all_to_all | solution.py:106
  395.4 479.5 %reduce-scatter.5.cloned.1.call-start = ((), (), s32[]{:S(2)}) async-start(), calls=%async_computation.8 | async-start | bytes 5242880 | tf_op jit(solution)/shard_map/reduce_scatter | solution.py:91
  398.1 148.7 %copy-start.2 = (f32[64,512,1,1]{1,0,2,3:T(8,128)}, f32[64,512,1,1]{1,0,2,3:T(8,128)S(1)}, u32[]{:S(2)}) copy-start(f32[64,512,1,1]{1,0,2,3:T(8,128)S(1)} %reshape.213) | copy-start | bytes 393220
  514.0 32.8 %copy-start.11 = (f32[32]{0:T(128)S(1)}, f32[32]{0:T(128)}, u32[]{:S(2)}) copy-start(f32[32]{0:T(128)} %param.10) | copy-start | bytes 388
  606.3 5.7 copy-start.1
  772.5 19.4 %copy-start.9 = (s32[32]{0:T(128)S(1)}, s32[32]{0:T(128)}, u32[]{:S(2)}) copy-start(s32[32]{0:T(128)} %copy-done.8) | copy-start | bytes 388
  791.9 18.9 %copy-start.7 = (f32[32,128]{1,0:T(8,128)S(1)}, f32[32,128]{1,0:T(8,128)}, u32[]{:S(2)}) copy-start(f32[32,128]{1,0:T(8,128)} %copy-done.6) | copy-start | bytes 49156
  828.7 112.4 %all-gather.5.cloned.1.call-start = ((), (), s32[]{:S(2)}) async-start(), calls=%async_computation.9 | async-start | bytes 5242880 | tf_op jit(solution)/shard_map/all_gather | solution.py:102
  991.9 155.3 %all-to-all-start.3 = ((f32[8,1,131072]{2,1,0:T(1,128)}), f32[8,1,131072]{2,1,0:T(1,128)}, u32[]{:S(2)}, u32[]{:S(2)}) async-start(f32[8,1,131072]{2,1,0:T(1,128)} %reshape.228), calls=%async_computation.5 | async-start | bytes 8388608 | tf_op jit(solution)/shard_map/all_to_all | solution.py:106
  997.4 112.3 %copy-start.4 = (f32[8,8,32,32]{3,2,1,0:T(8,128)S(1)}, f32[8,8,32,32]{3,2,1,0:T(8,128)}, u32[]{:S(2)}) copy-start(f32[8,8,32,32]{3,2,1,0:T(8,128)} %reduce-scatter.3.cloned.1.call-done) | copy-start | bytes 786436
  997.4 112.3 %copy-start.5 = (f32[8,8,32,32]{3,2,1,0:T(8,128)S(1)}, f32[8,8,32,32]{3,2,1,0:T(8,128)}, u32[]{:S(2)}) copy-start(f32[8,8,32,32]{3,2,1,0:T(8,128)} %reduce-scatter.5.cloned.1.call-done) | copy-start | bytes 786436
  1147.2 28.4 %copy-start.3 = (f32[64,512,1,1]{1,0,2,3:T(8,128)S(1)}, f32[64,512,1,1]{1,0,2,3:T(8,128)}, u32[]{:S(2)}) copy-start(f32[64,512,1,1]{1,0,2,3:T(8,128)} %copy-done.2) | copy-start | bytes 393220
Sparse Core Ops, SparseCore 0:
  239.8 46.2 reduce-scatter.2
  303.5 35.4 all-gather.2
  828.8 45.9 reduce-scatter.4
  905.6 35.4 all-gather.4
where the time goes:
time: 1250 us; the launch traced here: 1240 us
  waiting for transfers between devices  320 us (26%)
  matrix products  318 us (25%)
  local copies, waits for them, and re-layouts  301 us (24%)
  blocking collectives  195 us (16%)
  other arithmetic  71.6 us (6%)
  starting transfers between devices  16.9 us (1%)
  between operations  14.2 us (1%)
    unnamed x33, local copies, waits for them, and re-layouts  112 us
    psum x1, blocking collectives, local(): lax.psum((weight_local, bias_local), ('gx', 'gy'))  98.1 us
    all_to_all x1, blocking collectives, forward_modes(): lax.all_to_all(partial_depth, 'gx', split_axis=3, concat_axis=0, tiled=True)  96.7 us
    all_to_all x1, waiting for transfers between devices, forward_modes(): lax.all_to_all(partial_depth, 'gx', split_axis=3, concat_axis=0, tiled=True)  90.3 us
    all_to_all x2, waiting for transfers between devices, inverse_modes(): lax.all_to_all(planes, 'gx', split_axis=0, concat_axis=3, tiled=True)  87.1 us
    reduce_scatter x2, waiting for transfers between devices, forward_modes(): lax.psum_scatter(jnp.einsum('ky,jycm->kmjc', down_table, swept, precision...  71.7 us
    all_gather x2, waiting for transfers between devices, inverse_modes(): lax.all_gather(mode_block, 'gy', axis=0, tiled=True)  71.2 us
    dot_general x2, matrix products, inverse_modes(): jnp.dot(cell_modes.reshape(-1, cell_modes.shape[3]), depth_full, precisio...  65.3 us
  transfers between devices with their start and end apart: 7, of which 6 were waited for; matrix products, arithmetic and copies ran while one was open for 6% of the time, Pallas kernels for 0%

commit v1 on v0

v1 whole, which is shorter than its diff:
```python
import functools
import math

import jax
import jax.numpy as jnp
import ml_dtypes
import numpy as np
from jax import lax
from jax.experimental import pallas as pl
from jax.experimental.pallas import tpu as pltpu
from jax.sharding import PartitionSpec as P

LZ = 64
LT = 8
KZ = 16
KT = 4

keep_level = 6554
keep_scale = 1.0 / 0.9
gelu_cubic = 0.044715
mixer_one = -1640531535
mixer_two = -2048144789
mixer_three = -1028477387
low = jnp.bfloat16
wide = jnp.float32
VMEM_LIMIT = 56 * 1024 * 1024


def hartley_table(kept, length):
    wanted = np.arange(kept)
    frequency = np.where(wanted < kept // 2, wanted, wanted + (length - kept))
    residue = frequency[:, None] * np.arange(length)[None, :] % length
    radians = residue * (2.0 * math.pi / length)
    return (np.cos(radians) + np.sin(radians)) / math.sqrt(length)


def depth_table():
    depth_part = hartley_table(KZ, LZ)
    time_part = hartley_table(KT, LT)
    joined = depth_part[:, None, :, None] * time_part[None, :, None, :]
    return joined.reshape(KZ * KT, LZ * LT)


def low_constant(values):
    return jnp.asarray(np.asarray(values, np.float32).astype(ml_dtypes.bfloat16))


def low_pair(values):
    high = np.asarray(values, np.float32).astype(ml_dtypes.bfloat16)
    return jnp.asarray(high), low_constant(values - high.astype(np.float64))


def halves(values):
    high = values.astype(low)
    return high, (values - high.astype(wide)).astype(low)


def scramble(hashed):
    hashed = jnp.bitwise_xor(hashed, lax.shift_right_logical(hashed, jnp.int32(16)))
    hashed = hashed * jnp.int32(mixer_two)
    hashed = jnp.bitwise_xor(hashed, lax.shift_right_logical(hashed, jnp.int32(13)))
    hashed = hashed * jnp.int32(mixer_three)
    return jnp.bitwise_xor(hashed, lax.shift_right_logical(hashed, jnp.int32(16)))


def scaled_slope(preact):
    factor = math.sqrt(2.0 / math.pi)
    square = preact * preact
    tanh_value = jnp.tanh(preact * (square * (factor * gelu_cubic) + factor))
    inner = preact * (
        square * (0.5 * keep_scale * factor * 3.0 * gelu_cubic) + 0.5 * keep_scale * factor
    )
    return (1.0 + tanh_value) * (inner * (1.0 - tanh_value) + 0.5 * keep_scale)


def dot(a, b):
    return lax.dot_general(a, b, (((1,), (0,)), ((), ())), preferred_element_type=wide)


def dot_rows(a, b):
    return lax.dot_general(a, b, (((1,), (1,)), ((), ())), preferred_element_type=wide)


def dot_fine(a, b):
    return dot(a[0], b[0]) + (dot(a[1], b[0]) + dot(a[0], b[1]))


def forward_kernel(source_ref, depth_ref, down_ref, rest_ref, out_ref, swept, swept_rest):
    rows = source_ref.shape[0]
    modes = depth_ref.shape[0]
    lanes = out_ref.shape[3]
    for row in range(rows):
        window = slice(row * modes, (row + 1) * modes)
        swept[window, :], swept_rest[window, :] = halves(dot_rows(depth_ref[...], source_ref[row]))
    for part in range(out_ref.shape[0]):
        window = slice(part * lanes, (part + 1) * lanes)
        out_ref[part] = dot_fine(
            (swept[...], swept_rest[...]), (down_ref[:, window], rest_ref[:, window])
        ).reshape(rows, modes, lanes)


def forward_local(source, depth_low, down_wide, down_rest, parts):
    slab_rows, cells, depth_cells = source.shape
    modes = depth_low.shape[0]
    lanes = down_wide.shape[1] // parts
    step = min(4, slab_rows)
    return pl.pallas_call(
        forward_kernel,
        grid=(slab_rows // step,),
        in_specs=[
            pl.BlockSpec((step, cells, depth_cells), lambda i: (i, 0, 0)),
            pl.BlockSpec(depth_low.shape, lambda i: (0, 0)),
            pl.BlockSpec(down_wide.shape, lambda i: (0, 0)),
            pl.BlockSpec(down_rest.shape, lambda i: (0, 0)),
        ],
        out_specs=pl.BlockSpec((parts, step, modes, lanes), lambda i: (0, i, 0, 0)),
        out_shape=jax.ShapeDtypeStruct((parts, slab_rows, modes, lanes), wide),
        scratch_shapes=[pltpu.VMEM((step * modes, cells), low)] * 2,
        compiler_params=pltpu.CompilerParams(vmem_limit_bytes=VMEM_LIMIT),
        name="forward_local",
    )(source, depth_low, down_wide, down_rest)


def mix_kernel(
    planes_ref,
    weight_ref,
    across_ref,
    across_rest,
    back_ref,
    back_rest,
    pick_c,
    sum_d,
    modes_ref,
    out_ref,
    split,
    mixed,
):
    ky = pl.program_id(0)
    steps, _, channels = split.shape

    @pl.when(ky == 0)
    def _():
        modes = dot_fine((across_ref[...], across_rest[...]), halves(planes_ref[...]))
        modes_ref[...] = modes
        for part in range(steps):
            split[part] = modes[:, part * channels : (part + 1) * channels]

    high, rest = halves(split[ky])
    spread = dot(high, pick_c[...]) + dot(rest, pick_c[...])
    high, rest = halves(spread * weight_ref[0].astype(wide))
    mixed[ky] = dot(high, sum_d[...]) + dot(rest, sum_d[...])

    @pl.when(ky == steps - 1)
    def _():
        joined = jnp.concatenate([mixed[part] for part in range(steps)], axis=1)
        out_ref[...] = dot_fine((back_ref[...], back_rest[...]), halves(joined))


def mix_back_kernel(
    planes_ref,
    modes_ref,
    weight_ref,
    across_ref,
    back_ref,
    pick_c,
    pick_d,
    sum_c,
    grad_ref,
    out_ref,
    split_in,
    split,
    mixed,
):
    ky = pl.program_id(0)
    steps, _, channels = split.shape

    @pl.when(ky == 0)
    def _():
        modes = dot(across_ref[...], planes_ref[...].astype(low))
        for part in range(steps):
            window = slice(part * channels, (part + 1) * channels)
            split[part] = modes[:, window].astype(low)
            split_in[part] = modes_ref[:, window].astype(low)

    spread = dot(split[ky], pick_d[...])
    grad_ref[0] = dot(split_in[ky], pick_c[...]) * spread
    product = spread.astype(low) * weight_ref[0]
    mixed[ky] = dot(product, sum_c[...]).astype(low)

    @pl.when(ky == steps - 1)
    def _():
        joined = jnp.concatenate([mixed[part] for part in range(steps)], axis=1)
        out_ref[...] = dot(back_ref[...], joined)


def whole_spec(array):
    return pl.BlockSpec(array.shape, lambda i: (0,) * array.ndim)


def mix_modes(planes, weight, across, across_rest, back, back_rest, pick_c, sum_d):
    kept_rows, lanes = across.shape[0], planes.shape[1]
    steps, _, pairs = weight.shape
    channels = lanes // steps
    return pl.pallas_call(
        mix_kernel,
        grid=(steps,),
        in_specs=[
            whole_spec(planes),
            pl.BlockSpec((1, kept_rows, pairs), lambda i: (i, 0, 0)),
            whole_spec(across),
            whole_spec(across_rest),
            whole_spec(back),
            whole_spec(back_rest),
            whole_spec(pick_c),
            whole_spec(sum_d),
        ],
        out_specs=[
            pl.BlockSpec((kept_rows, lanes), lambda i: (0, 0)),
            pl.BlockSpec(planes.shape, lambda i: (0, 0)),
        ],
        out_shape=[
            jax.ShapeDtypeStruct((kept_rows, lanes), wide),
            jax.ShapeDtypeStruct(planes.shape, wide),
        ],
        scratch_shapes=[
            pltpu.VMEM((steps, kept_rows, channels), wide),
            pltpu.VMEM((steps, kept_rows, channels), wide),
        ],
        compiler_params=pltpu.CompilerParams(vmem_limit_bytes=VMEM_LIMIT),
        name="mix_modes",
    )(planes, weight, across, across_rest, back, back_rest, pick_c, sum_d)


def mix_back(planes, modes, weight, across, back, pick_c, pick_d, sum_c):
    kept_rows, lanes = across.shape[0], planes.shape[1]
    steps, _, pairs = weight.shape
    channels = lanes // steps
    return pl.pallas_call(
        mix_back_kernel,
        grid=(steps,),
        in_specs=[
            whole_spec(planes),
            whole_spec(modes),
            pl.BlockSpec((1, kept_rows, pairs), lambda i: (i, 0, 0)),
            whole_spec(across),
            whole_spec(back),
            whole_spec(pick_c),
            whole_spec(pick_d),
            whole_spec(sum_c),
        ],
        out_specs=[
            pl.BlockSpec((1, kept_rows, pairs), lambda i: (i, 0, 0)),
            pl.BlockSpec(planes.shape, lambda i: (0, 0)),
        ],
        out_shape=[
            jax.ShapeDtypeStruct((steps, kept_rows, pairs), wide),
            jax.ShapeDtypeStruct(planes.shape, wide),
        ],
        scratch_shapes=[
            pltpu.VMEM((steps, kept_rows, channels), low),
            pltpu.VMEM((steps, kept_rows, channels), low),
            pltpu.VMEM((steps, kept_rows, channels), low),
        ],
        compiler_params=pltpu.CompilerParams(vmem_limit_bytes=VMEM_LIMIT),
        name="mix_back",
    )(planes, modes, weight, across, back, pick_c, pick_d, sum_c)


def joined_parts(gathered_ref):
    parts, devices, rows, owned, lanes = gathered_ref.shape
    return jnp.concatenate(
        [
            jnp.concatenate(
                [gathered_ref[part, :, row].reshape(devices * owned, lanes) for row in range(rows)],
                axis=0,
            )
            for part in range(parts)
        ],
        axis=1,
    )


def column_modes(gathered_ref, up_ref, turned):
    rows, _, modes = turned.shape
    columns = dot(joined_parts(gathered_ref).astype(low), up_ref[...])
    for row in range(rows):
        turned[row] = columns[row * modes : (row + 1) * modes, :].T.astype(low)


def column_modes_fine(gathered_ref, up_ref, up_rest, turned):
    rows, _, stacked = turned.shape
    modes = stacked // 3
    columns = dot_fine(halves(joined_parts(gathered_ref)), (up_ref[...], up_rest[...]))
    for row in range(rows):
        high, rest = halves(columns[row * modes : (row + 1) * modes, :].T)
        turned[row] = jnp.concatenate([high, rest, high], axis=1)


def middle_kernel(
    channels,
    gathered_ref,
    source_ref,
    cotangent_ref,
    up_ref,
    up_rest,
    depth_ref,
    depth_low_ref,
    down_ref,
    bypass_ref,
    bias_ref,
    dpre_ref,
    modes_ref,
    weight_ref,
    sums_ref,
    turned,
    preact,
    swept,
):
    step = pl.program_id(0)
    rows, cells, depth_cells = source_ref.shape
    modes = depth_low_ref.shape[0]
    lanes = modes_ref.shape[3]
    block = bypass_ref.shape[0]
    columns = cells // channels

    @pl.when(step == 0)
    def _():
        weight_ref[...] = jnp.zeros_like(weight_ref)
        sums_ref[...] = jnp.zeros_like(sums_ref)

    column_modes_fine(gathered_ref, up_ref, up_rest, turned)
    for row in range(rows):
        for start in range(0, cells, block):
            window = slice(start, start + block)
            preact[window, :] = dot(turned[row, window, :], depth_ref[...]) + dot(
                bypass_ref[...], source_ref[row, window, :]
            )
        def one_column(column, carry):
            start = pl.multiple_of(column * channels, channels)
            window = pl.ds(start, channels)
            slope = scaled_slope(preact[window, :] + bias_ref[...])
            value = cotangent_ref[row, window, :].astype(wide) * slope
            dpre_ref[row, window, :] = value.astype(low)
            return carry

        lax.fori_loop(0, columns, one_column, 0)
        depth_sums = dot_rows(depth_low_ref[...], dpre_ref[row])
        sums_ref[...] += depth_sums[:8, :]
        swept[row * modes : (row + 1) * modes, :] = depth_sums.astype(low)
        total = weight_ref[...]
        for start in range(0, cells, block):
            window = slice(start, start + block)
            total += dot_rows(source_ref[row, window, :], dpre_ref[row, window, :])
        weight_ref[...] = total
    for part in range(modes_ref.shape[0]):
        modes_ref[part] = dot(
            swept[...], down_ref[:, part * lanes : (part + 1) * lanes]
        ).reshape(rows, modes, lanes)


def middle_pass(
    gathered, source, cotangent, up, up_rest, depth, depth_low, down, bypass, bias
):
    parts, devices, slab_rows, owned, lanes = gathered.shape
    modes = devices * owned
    _, cells, depth_cells = source.shape
    channels = bias.shape[0]
    block = bypass.shape[0]
    step = min(4, slab_rows)
    row_spec = pl.BlockSpec((step, cells, depth_cells), lambda i: (i, 0, 0))
    part_spec = pl.BlockSpec((parts, step, modes, lanes), lambda i: (0, i, 0, 0))
    return pl.pallas_call(
        functools.partial(middle_kernel, channels),
        grid=(slab_rows // step,),
        in_specs=[
            pl.BlockSpec((parts, devices, step, owned, lanes), lambda i: (0, 0, i, 0, 0)),
            row_spec,
            row_spec,
            whole_spec(up),
            whole_spec(up_rest),
            whole_spec(depth),
            whole_spec(depth_low),
            whole_spec(down),
            whole_spec(bypass),
            whole_spec(bias),
        ],
        out_specs=[
            row_spec,
            part_spec,
            pl.BlockSpec((block, block), lambda i: (0, 0)),
            pl.BlockSpec((8, cells), lambda i: (0, 0)),
        ],
        out_shape=[
            jax.ShapeDtypeStruct(source.shape, low),
            jax.ShapeDtypeStruct((parts, slab_rows, modes, lanes), wide),
            jax.ShapeDtypeStruct((block, block), wide),
            jax.ShapeDtypeStruct((8, cells), wide),
        ],
        scratch_shapes=[
            pltpu.VMEM((step, cells, 3 * modes), low),
            pltpu.VMEM((cells, depth_cells), wide),
            pltpu.VMEM((step * modes, cells), low),
        ],
        compiler_params=pltpu.CompilerParams(vmem_limit_bytes=VMEM_LIMIT),
        name="middle_pass",
    )(gathered, source, cotangent, up, up_rest, depth, depth_low, down, bypass, bias)


def last_kernel(gathered_ref, dpre_ref, up_ref, depth_ref, bypass_ref, out_ref, turned):
    rows, cells, _ = dpre_ref.shape
    block = bypass_ref.shape[0]
    column_modes(gathered_ref, up_ref, turned)
    for row in range(rows):
        for start in range(0, cells, block):
            window = slice(start, start + block)
            out_ref[row, window, :] = (
                dot(turned[row, window, :], depth_ref[...])
                + dot(bypass_ref[...], dpre_ref[row, window, :])
            ).astype(low)


def last_pass(gathered, dpre, up, depth, bypass):
    parts, devices, slab_rows, owned, lanes = gathered.shape
    modes = devices * owned
    _, cells, depth_cells = dpre.shape
    step = min(4, slab_rows)
    row_spec = pl.BlockSpec((step, cells, depth_cells), lambda i: (i, 0, 0))
    return pl.pallas_call(
        last_kernel,
        grid=(slab_rows // step,),
        in_specs=[
            pl.BlockSpec((parts, devices, step, owned, lanes), lambda i: (0, 0, i, 0, 0)),
            row_spec,
            whole_spec(up),
            whole_spec(depth),
            whole_spec(bypass),
        ],
        out_specs=row_spec,
        out_shape=jax.ShapeDtypeStruct(dpre.shape, low),
        scratch_shapes=[pltpu.VMEM((step, cells, modes), low)],
        compiler_params=pltpu.CompilerParams(vmem_limit_bytes=VMEM_LIMIT),
        name="last_pass",
    )(gathered, dpre, up, depth, bypass)


MESH = pl.DeviceIdType.MESH


def neighbours():
    row, column = lax.axis_index("gx"), lax.axis_index("gy")
    core, side = column % 2, column // 2
    return row, column, side * 2 + 1 - core, (1 - side) * 2 + core


def greet(row, column, mate, across):
    row_devices = lax.axis_size("gx")
    barrier = pltpu.get_barrier_semaphore()
    for target in (mate, across):
        pl.semaphore_signal(barrier, inc=1, device_id=(row, target), device_id_type=MESH)

    def signal_peer(offset, carry):
        pl.semaphore_signal(
            barrier,
            inc=1,
            device_id=(lax.rem(row + offset, row_devices), column),
            device_id_type=MESH,
        )
        return carry

    lax.fori_loop(1, row_devices, signal_peer, 0)
    pl.semaphore_wait(barrier, row_devices + 1)


def send(source, target, semaphores, at, device):
    return pltpu.make_async_remote_copy(
        src_ref=source,
        dst_ref=target,
        send_sem=semaphores.at[(0, *at)],
        recv_sem=semaphores.at[(1, *at)],
        device_id=device,
        device_id_type=MESH,
    )


def to_owner_steps(partial_ref, out_ref, mate_in, across_out, across_in, peer_out, sems):
    mate_sem, across_sem, peer_sem = sems
    _, slab_rows, _, _ = partial_ref.shape
    row, column, mate, across = neighbours()
    core, side = column % 2, column // 2
    row_devices, owned = peer_out.shape[0], peer_out.shape[2]
    chunks = mate_sem.shape[2]
    rows = slab_rows // chunks

    def window(chunk):
        return pl.ds(chunk * rows, rows)

    def mate_copy(chunk, half):
        return send(
            partial_ref.at[half * 2 + 1 - core, window(chunk)],
            mate_in.at[half, window(chunk)],
            mate_sem,
            (half, chunk),
            (row, mate),
        )

    def across_copy(chunk):
        return send(
            across_out.at[window(chunk)],
            across_in.at[window(chunk)],
            across_sem,
            (chunk,),
            (row, across),
        )

    def peer_copy(chunk, offset):
        peer = lax.rem(row + offset, row_devices)
        return send(
            peer_out.at[peer, window(chunk)],
            out_ref.at[row, window(chunk)],
            peer_sem,
            (chunk, offset - 1),
            (peer, column),
        )

    def start(chunk):
        for half in range(2):
            mate_copy(chunk, half).start()

    def pair_sum(chunk):
        for half in range(2):
            mate_copy(chunk, half).wait_recv()
        across_out[window(chunk)] = (
            partial_ref[across, window(chunk)] + mate_in[1 - side, window(chunk)]
        )
        across_copy(chunk).start()

    def side_sum(chunk):
        across_copy(chunk).wait_recv()
        total = (
            partial_ref[column, window(chunk)] + mate_in[side, window(chunk)]
        ) + across_in[window(chunk)]
        for peer in range(row_devices):
            peer_out[peer, window(chunk)] = total[:, peer * owned : (peer + 1) * owned, :]

        def start_peer(offset, carry):
            peer_copy(chunk, offset).start()
            return carry

        lax.fori_loop(1, row_devices, start_peer, 0)
        out_ref[row, window(chunk)] = peer_out[row, window(chunk)]

    def finish():
        for chunk in range(chunks):

            def wait_peer(offset, carry):
                copy = peer_copy(chunk, offset)
                copy.wait_recv()
                copy.wait_send()
                return carry

            lax.fori_loop(1, row_devices, wait_peer, 0)
            across_copy(chunk).wait_send()
            for half in range(2):
                mate_copy(chunk, half).wait_send()

    return chunks, start, pair_sum, side_sum, finish


def to_owner_kernel(partial_ref, out_ref, mate_in, across_out, across_in, peer_out, *sems):
    greet(*neighbours())
    chunks, start, pair_sum, side_sum, finish = to_owner_steps(
        partial_ref, out_ref, mate_in, across_out, across_in, peer_out, sems
    )
    for chunk in range(chunks):
        start(chunk)
    for chunk in range(chunks):
        pair_sum(chunk)
    for chunk in range(chunks):
        side_sum(chunk)
    finish()


def masking_kernel(
    all_columns,
    channels,
    key_ref,
    partial_ref,
    cotangent_ref,
    out_ref,
    masked_ref,
    mate_in,
    across_out,
    across_in,
    peer_out,
    held,
    made,
    offsets,
    in_sem,
    out_sem,
    *sems,
):
    slab_rows, cells, depth_cells = cotangent_ref.shape
    columns = cells // channels

    def fetch(row):
        return pltpu.make_async_copy(
            cotangent_ref.at[row], held.at[row % 2], in_sem.at[row % 2]
        )

    def put(row):
        return pltpu.make_async_copy(made.at[row % 2], masked_ref.at[row], out_sem.at[row % 2])

    fetch(0).start()
    offsets[...] = (
        lax.broadcasted_iota(jnp.int32, offsets.shape, 0) * depth_cells
        + lax.broadcasted_iota(jnp.int32, offsets.shape, 1)
    ) * jnp.int32(mixer_one)
    greet(*neighbours())
    chunks, start, pair_sum, side_sum, finish = to_owner_steps(
        partial_ref, out_ref, mate_in, across_out, across_in, peer_out, sems
    )
    for chunk in range(chunks):
        start(chunk)
    plan = {row: [] for row in range(slab_rows)}
    for chunk in range(chunks):
        plan[min(chunk, slab_rows - 1)].append((pair_sum, chunk))
    for chunk in range(chunks):
        plan[min(slab_rows - 1, (chunk + 1) * slab_rows // chunks)].append((side_sum, chunk))
    row_base = lax.axis_index("gx") * slab_rows
    column_base = lax.axis_index("gy") * columns
    stride = (channels * depth_cells * mixer_one + 2**31) % 2**32 - 2**31
    for row in range(slab_rows):
        if row + 1 < slab_rows:
            fetch(row + 1).start()
        fetch(row).wait()
        if row >= 2:
            put(row - 2).wait()
        first = ((row_base + row) * all_columns + column_base) * jnp.int32(stride) + key_ref[0]

        def one_column(column, carry):
            window = pl.ds(pl.multiple_of(column * channels, channels), channels)
            hashed = scramble(offsets[...] + (first + column * jnp.int32(stride)))
            hashed = scramble(jnp.bitwise_xor(hashed, key_ref[1]))
            keep = jnp.bitwise_and(hashed, jnp.int32(65535)) >= keep_level
            made[row % 2, window, :] = jnp.where(
                keep, held[row % 2, window, :].astype(wide), 0.0
            ).astype(low)
            return carry

        lax.fori_loop(0, columns, one_column, 0)
        put(row).start()
        for step, chunk in plan[row]:
            step(chunk)
    for row in range(max(0, slab_rows - 2), slab_rows):
        put(row).wait()
    finish()


def owner_scratch(partial, row_devices):
    parts, slab_rows, modes, lanes = partial.shape
    owned = modes // row_devices
    chunks = min(4, slab_rows)
    return jax.ShapeDtypeStruct((row_devices, slab_rows, owned, lanes), wide), [
        pltpu.VMEM((2, slab_rows, modes, lanes), wide),
        pltpu.VMEM((slab_rows, modes, lanes), wide),
        pltpu.VMEM((slab_rows, modes, lanes), wide),
        pltpu.VMEM((row_devices, slab_rows, owned, lanes), wide),
    ], [
        pltpu.SemaphoreType.DMA((2, 2, chunks)),
        pltpu.SemaphoreType.DMA((2, chunks)),
        pltpu.SemaphoreType.DMA((2, chunks, row_devices - 1)),
    ]


vmem_spec = pl.BlockSpec(memory_space=pltpu.VMEM)


def to_owner(partial):
    shape, buffers, sems = owner_scratch(partial, lax.axis_size("gx"))
    planes = pl.pallas_call(
        to_owner_kernel,
        in_specs=[vmem_spec],
        out_specs=vmem_spec,
        out_shape=shape,
        scratch_shapes=buffers + sems,
        compiler_params=pltpu.CompilerParams(
            collective_id=0, has_side_effects=True, vmem_limit_bytes=VMEM_LIMIT
        ),
        name="to_owner",
    )(partial)
    return planes.reshape(-1, planes.shape[3])


def to_owner_masking(partial, cotangent, hash_key, channels, all_columns):
    shape, buffers, sems = owner_scratch(partial, lax.axis_size("gx"))
    _, cells, depth_cells = cotangent.shape
    planes, masked = pl.pallas_call(
        functools.partial(masking_kernel, all_columns, channels),
        in_specs=[
            pl.BlockSpec(memory_space=pltpu.SMEM),
            vmem_spec,
            pl.BlockSpec(memory_space=pl.ANY),
        ],
        out_specs=[vmem_spec, pl.BlockSpec(memory_space=pl.ANY)],
        out_shape=[shape, jax.ShapeDtypeStruct(cotangent.shape, low)],
        scratch_shapes=buffers
        + [
            pltpu.VMEM((2, cells, depth_cells), low),
            pltpu.VMEM((2, cells, depth_cells), low),
            pltpu.VMEM((channels, depth_cells), jnp.int32),
            pltpu.SemaphoreType.DMA((2,)),
            pltpu.SemaphoreType.DMA((2,)),
        ]
        + sems,
        compiler_params=pltpu.CompilerParams(
            collective_id=1, has_side_effects=True, vmem_limit_bytes=VMEM_LIMIT
        ),
        name="to_owner_masking",
    )(hash_key, partial, cotangent)
    return planes.reshape(-1, planes.shape[3]), masked


def from_owner_kernel(spread_ref, out_ref, peer_sem, across_sem, mate_sem):
    row, column, mate, across = neighbours()
    row_devices, slab_rows = spread_ref.shape[:2]
    chunks = peer_sem.shape[1]
    rows = slab_rows // chunks
    greet(row, column, mate, across)

    def window(chunk):
        return pl.ds(chunk * rows, rows)

    def peer_copy(chunk, offset):
        peer = lax.rem(row + offset, row_devices)
        return send(
            spread_ref.at[peer, window(chunk)],
            out_ref.at[column, row, window(chunk)],
            peer_sem,
            (chunk, offset - 1),
            (peer, column),
        )

    def part_copy(chunk, part, sem, at, target):
        view = out_ref.at[part, :, window(chunk)]
        return send(view, view, sem, at, (row, target))

    def across_copy(chunk):
        return part_copy(chunk, column, across_sem, (chunk,), across)

    def mate_copy(chunk, half):
        return part_copy(chunk, across if half else column, mate_sem, (half, chunk), mate)

    for chunk in range(chunks):

        def start_peer(offset, carry):
            peer_copy(chunk, offset).start()
            return carry

        lax.fori_loop(1, row_devices, start_peer, 0)
    out_ref[column, row] = spread_ref[row]
    for chunk in range(chunks):

        def wait_peer(offset, carry):
            peer_copy(chunk, offset).wait_recv()
            return carry

        lax.fori_loop(1, row_devices, wait_peer, 0)
        across_copy(chunk).start()
        mate_copy(chunk, 0).start()
    for chunk in range(chunks):
        across_copy(chunk).wait_recv()
        mate_copy(chunk, 1).start()
    for chunk in range(chunks):
        for half in range(2):
            mate_copy(chunk, half).wait()
        across_copy(chunk).wait_send()

        def wait_sent(offset, carry):
            peer_copy(chunk, offset).wait_send()
            return carry

        lax.fori_loop(1, row_devices, wait_sent, 0)


def from_owner(planes, kept):
    row_devices = lax.axis_size("gx")
    spread = planes.reshape(row_devices, -1, kept, planes.shape[1])
    slab_rows = spread.shape[1]
    chunks = min(4, slab_rows)
    return pl.pallas_call(
        from_owner_kernel,
        in_specs=[vmem_spec],
        out_specs=vmem_spec,
        out_shape=jax.ShapeDtypeStruct((lax.axis_size("gy"), *spread.shape), wide),
        scratch_shapes=[
            pltpu.SemaphoreType.DMA((2, chunks, row_devices - 1)),
            pltpu.SemaphoreType.DMA((2, chunks)),
            pltpu.SemaphoreType.DMA((2, 2, chunks)),
        ],
        compiler_params=pltpu.CompilerParams(
            collective_id=2, has_side_effects=True, vmem_limit_bytes=VMEM_LIMIT
        ),
        name="from_owner",
    )(spread)


def local(layer_input, cotangent, spectral_weight, bypass_weight, channel_bias, hash_key):
    slab_rows, slab_columns, channels, depth_cells = layer_input.shape
    row_devices = lax.axis_size("gx")
    column_devices = lax.axis_size("gy")
    owned_columns, owned_modes, kept_rows, pairs = spectral_weight.shape
    all_rows = slab_rows * row_devices
    all_columns = slab_columns * column_devices
    kept_columns = owned_columns * column_devices
    column_offset = lax.axis_index("gy") * slab_columns
    cells = slab_columns * channels

    one_channel = np.eye(channels)
    down = hartley_table(kept_columns, all_columns)
    down_all = low_pair(np.kron(down.T, one_channel))
    up_all = low_pair(
        np.kron(
            down.reshape(kept_columns, column_devices, slab_columns).transpose(1, 0, 2), one_channel
        )
    )
    down_wide, down_rest = (
        lax.dynamic_slice_in_dim(table, column_offset * channels, cells, 0) for table in down_all
    )
    up_wide, up_rest = (
        lax.dynamic_index_in_dim(table, lax.axis_index("gy"), 0, keepdims=False)
        for table in up_all
    )
    across = hartley_table(kept_rows, all_rows)
    one_mode = np.eye(owned_modes)
    across_wide = np.einsum("kx,mn->mkxn", across, one_mode).reshape(
        owned_modes * kept_rows, all_rows * owned_modes
    )
    back_wide, back_rest = low_pair(across_wide.T)
    across_wide, across_rest = low_pair(across_wide)
    pick_c = np.kron(one_channel, np.ones((1, channels)))
    pick_d = np.kron(np.ones((1, channels)), one_channel)
    sum_c, sum_d = low_constant(pick_c.T), low_constant(pick_d.T)
    pick_c, pick_d = low_constant(pick_c), low_constant(pick_d)
    depth_low, depth_rest = low_pair(depth_table())
    depth_stack = jnp.concatenate([depth_low, depth_low, depth_rest], axis=0)
    group = max(1, 256 // channels)
    one_group = jnp.eye(group, dtype=low)
    bypass_in = jnp.kron(one_group, bypass_weight.T)
    bypass_out = jnp.kron(one_group, bypass_weight)

    source = layer_input.reshape(slab_rows, cells, depth_cells)
    weight = spectral_weight.reshape(owned_columns, owned_modes * kept_rows, pairs)

    planes, masked = to_owner_masking(
        forward_local(source, depth_low, down_wide, down_rest, column_devices),
        cotangent.reshape(source.shape),
        hash_key,
        channels,
        all_columns,
    )
    input_modes, spread = mix_modes(
        planes, weight, across_wide, across_rest, back_wide, back_rest, pick_c, sum_d
    )
    dpre, partial, weight_local, sums_local = middle_pass(
        from_owner(spread, owned_modes),
        source,
        masked,
        up_wide,
        up_rest,
        depth_stack,
        depth_low,
        down_wide,
        bypass_in,
        channel_bias[:, None],
    )
    weight_local = jnp.einsum(
        "acad->cd", weight_local.reshape(group, channels, group, channels)
    )
    bias_local = jnp.sum(sums_local[0].reshape(slab_columns, channels), axis=0) / depth_low[
        0, 0
    ].astype(wide)
    weight_total, bias_total = lax.psum((weight_local, bias_local), ("gx", "gy"))
    norm_scale = 1.0 / math.sqrt(all_rows * all_columns * depth_cells)
    grad_spectral, spread_back = mix_back(
        to_owner(partial), input_modes, weight, across_wide, back_wide, pick_c, pick_d, sum_c
    )
    grad_input = last_pass(
        from_owner(spread_back, owned_modes), dpre, up_wide, depth_low, bypass_out
    )
    return (
        grad_input.reshape(layer_input.shape),
        grad_spectral.reshape(spectral_weight.shape),
        weight_total * norm_scale,
        bias_total * norm_scale,
    )


def solution(mesh):
    return jax.shard_map(
        local,
        mesh=mesh,
        in_specs=(
            P("gx", "gy", None, None),
            P("gx", "gy", None, None),
            P("gy", "gx", None, None),
            P(),
            P(),
            P(),
        ),
        out_specs=(P("gx", "gy", None, None), P("gy", "gx", None, None), P(), P()),
        check_vma=False,
    )
```

time: 1250 us -> 384 us (0.31); the launches traced: 1240 us -> 384 us
  Pallas kernels: 0 us -> 325 us
  waiting for transfers between devices: 320 us -> 0 us
  matrix products: 318 us -> 0 us
  local copies, waits for them, and re-layouts: 301 us -> 15.5 us
  blocking collectives: 195 us -> 40 us
  other arithmetic: 71.6 us -> 2.2 us
  starting transfers between devices: 16.9 us -> 0 us
  between operations: 14.2 us -> 0.71 us
    pallas_call x0 -> x9, Pallas kernels: none -> 325 us  [the longest x1 95.8 us: middle_pass(): pl.pallas_call(functools.partial(middle_kernel, channels), grid=(slab_row...]
    dot_general x17 -> x0, matrix products: 318 us -> none  [the longest x2 65.3 us: inverse_modes(): jnp.dot(cell_modes.reshape(-1, cell_modes.shape[3]), depth_full, precisio...]
    all_to_all x3 -> x0, waiting for transfers between devices: 177 us -> none  [the longest x1 90.3 us: forward_modes(): lax.all_to_all(partial_depth, 'gx', split_axis=3, concat_axis=0, tiled=True)]
    unnamed x33 -> x0, local copies, waits for them, and re-layouts: 112 us -> none
    all_to_all x1 -> x0, blocking collectives: 96.7 us -> none  [forward_modes(): lax.all_to_all(partial_depth, 'gx', split_axis=3, concat_axis=0, tiled=True)]
    reduce_scatter x2 -> x0, waiting for transfers between devices: 71.7 us -> none  [forward_modes(): lax.psum_scatter(jnp.einsum('ky,jycm->kmjc', down_table, swept, precision...]
    all_gather x2 -> x0, waiting for transfers between devices: 71.2 us -> none  [inverse_modes(): lax.all_gather(mode_block, 'gy', axis=0, tiled=True)]
    all_to_all x4 -> x0, other arithmetic: 58.5 us -> none  [the longest x2 29.3 us: forward_modes(): lax.all_to_all(partial_depth, 'gx', split_axis=3, concat_axis=0, tiled=True)]
  transfers between devices with their start and end apart: 7 -> 0, of which waited for: 6 -> 0; matrix products, arithmetic and copies ran while one was open for 6% -> 0% of each run, Pallas kernels for 0% -> 0%
where the time goes in v1:
time: 384 us
  Pallas kernels  325 us (85%)
  blocking collectives  40 us (10%)
  local copies, waits for them, and re-layouts  15.5 us (4%)
    pallas_call x1, Pallas kernels, middle_pass(): pl.pallas_call(functools.partial(middle_kernel, channels), grid=(slab_row...  95.8 us
    pallas_call x2, Pallas kernels, from_owner(): pl.pallas_call(from_owner_kernel, in_specs=[vmem_spec], out_specs=vmem_sp...  89 us
    pallas_call x1, Pallas kernels, to_owner_masking(): pl.pallas_call(functools.partial(masking_kernel, all_columns, channels),...  44.2 us
    psum x1, blocking collectives, local(): lax.psum((weight_local, bias_local), ('gx', 'gy'))  40 us
    pallas_call x1, Pallas kernels, to_owner(): pl.pallas_call(to_owner_kernel, in_specs=[vmem_spec], out_specs=vmem_spec...  38.2 us
    pallas_call x1, Pallas kernels, last_pass(): pl.pallas_call(last_kernel, grid=(slab_rows // step,), in_specs=[pl.Block...  18.4 us
    pallas_call x1, Pallas kernels, forward_local(): pl.pallas_call(forward_kernel, grid=(slab_rows // step,), in_specs=[pl.Bl...  16.7 us
    pallas_call x1, Pallas kernels, mix_modes(): pl.pallas_call(mix_kernel, grid=(steps,), in_specs=[whole_spec(planes), p...  11.7 us

profile of v1, /device:TPU:13, one launch (start us, length us, event | category | flops | bytes accessed | tf_op | source)
XLA Modules:
  0.0 383.6 jit_solution(10005048703590562550)
XLA Ops:
  0.7 0.8 copy.24
  1.4 1.3 copy.25.bias_ref
  2.8 0.8 broadcast_multiply_fusion
  3.6 1.0 mul.65.bypass_ref
  4.6 1.0 mul.62.bypass_ref
  5.7 4.7 %constant_dynamic-slice_fusion = (bf16[1024,1024]{1,0:T(8,128)(2,1)}, bf16[1024,1024]{1,0:T(8,128)(2,1)}) fusion(bf16[4096,1024]{1,0:T(8,128)(2,1)} %constant.53.clone, s32[]{:T(128)S(6)} %select_n.12, bf16[4096,1024]{1,0:T(8,128)(2,1)} %constant.52.clone), kind=kLoop, calls=%fused_computation.10 | loop fusion | bytes 8388612 | tf_op jit(solution)/shard_map/dynamic_slice | solution.py:827
  10.3 16.7 %forward_local.1.partial_ref = f32[4,16,64,256]{3,2,1,0:T(8,128)} custom-call(bf16[16,1024,512]{2,1,0:T(8,128)(2,1)} %bitcast.19, bf16[64,512]{1,0:T(8,128)(2,1)} %constant.64.clone.depth_ref.depth_low_ref, bf16[1024,1024]{1,0:T(8,128)(2,1)} %get-tuple-element.29.down_ref, bf16[1024,1024]{1,0:T(8,128)(2,1)} %get-tuple-element.28.rest_ref), custom_call_target="tpu_custom_call" | custom-call | tf_op jit(solution)/shard_map/forward_local/pallas_call | solution.py:107
  27.0 4.7 %dynamic-slice_bitcast_fusion = (bf16[1024,1024]{1,0:T(8,128)(2,1)}, bf16[1024,1024]{1,0:T(8,128)(2,1)}) fusion(bf16[4,1024,1024]{2,1,0:T(8,128)(2,1)} %constant.55.clone, s32[]{:T(128)S(6)} %select_n.13, bf16[4,1024,1024]{2,1,0:T(8,128)(2,1)} %constant.54.clone), kind=kLoop, calls=%fused_computation | loop fusion | bytes 8388612 | tf_op jit(solution)/shard_map/jit(dynamic_index_in_dim)/squeeze | solution.py:830
  31.7 44.2 %to_owner_masking.1 = (f32[8,16,8,256]{3,2,1,0:T(8,128)}, bf16[16,1024,512]{2,1,0:T(8,128)(2,1)}) custom-call(s32[2]{0:T(128)} %key_ref.1, f32[4,16,64,256]{3,2,1,0:T(8,128)} %forward_local.1.partial_ref, bf16[16,1024,512]{2,1,0:T(8,128)(2,1)} %bitcast.22), custom_call_target="tpu_custom_call" | custom-call | tf_op jit(solution)/shard_map/to_owner_masking/pallas_call | solution.py:697
  75.9 11.7 %mix_modes.1 = (f32[256,256]{1,0:T(8,128)}, f32[1024,256]{1,0:T(8,128)}) custom-call(f32[1024,256]{1,0:T(8,128)} %bitcast.28, bf16[8,256,1024]{2,1,0:T(8,128)(2,1)} %bitcast.23, bf16[256,1024]{1,0:T(8,128)(2,1)} %constant.58.clone.across_ref, bf16[256,1024]{1,0:T(8,128)(2,1)} %constant.59.clone.across_rest, bf16[1024,256]{1,0:T(8,128)(2,1)} %constant.56.clone.back_ref, ...), custom_call_target="tpu_custom_call" | custom-call | tf_op jit(solution)/shard_map/mix_modes/pallas_call | solution.py:204
  87.5 43.3 %from_owner.2.gathered_ref = f32[4,8,16,8,256]{4,3,2,1,0:T(8,128)} custom-call(f32[8,16,8,256]{3,2,1,0:T(8,128)} %bitcast.27), custom_call_target="tpu_custom_call" | custom-call | tf_op jit(solution)/shard_map/from_owner/pallas_call | solution.py:790
  130.8 95.8 %middle_pass.1 = (bf16[16,1024,512]{2,1,0:T(8,128)(2,1)}, f32[4,16,64,256]{3,2,1,0:T(8,128)}, f32[256,256]{1,0:T(8,128)}, f32[8,1024]{1,0:T(8,128)}) custom-call(f32[4,8,16,8,256]{4,3,2,1,0:T(8,128)} %from_owner.2.gathered_ref, bf16[16,1024,512]{2,1,0:T(8,128)(2,1)} %bitcast.20, bf16[16,1024,512]{2,1,0:T(8,128)(2,1)} %get-tuple-element.16.cotangent_ref, ...), custom_call_target="tpu_custom_call" | custom-call | tf_op jit(solution)/shard_map/middle_pass/pallas_call | solution.py:372
  226.6 38.2 %to_owner.1 = f32[8,16,8,256]{3,2,1,0:T(8,128)} custom-call(f32[4,16,64,256]{3,2,1,0:T(8,128)} %get-tuple-element.17.partial_ref), custom_call_target="tpu_custom_call" | custom-call | tf_op jit(solution)/shard_map/to_owner/pallas_call | solution.py:680
  264.8 0.8 slice_reduce_fusion
  265.6 0.1 reshape_squeeze.3
  265.7 1.2 reshape.68
  266.9 0.2 select_reduce_fusion
  267.1 40.0 %all-reduce = (f32[32,32]{1,0:T(8,128)S(1)}, f32[32]{0:T(128)S(1)}) all-reduce(f32[32,32]{1,0:T(8,128)S(1)} %select_reduce_fusion, f32[32]{0:T(128)S(1)} %broadcast_multiply_fusion.3), channel_id=1, replica_groups=mesh['gx'=8,'gy'=4] {'gx','gy'}, use_global_device_ids=true, to_apply=%region_1.2 | all-reduce | flops 1056 | bytes 8448 | tf_op jit(solution)/shard_map/psum | solution.py:882
  307.1 0.6 broadcast_multiply_fusion.2
  307.7 0.5 broadcast_multiply_fusion.4
  308.2 11.3 %mix_back.1 = (f32[8,256,1024]{2,1,0:T(8,128)}, f32[1024,256]{1,0:T(8,128)}) custom-call(f32[1024,256]{1,0:T(8,128)} %bitcast.25, f32[256,256]{1,0:T(8,128)} %get-tuple-element.18.modes_ref, bf16[8,256,1024]{2,1,0:T(8,128)(2,1)} %bitcast.24, bf16[256,1024]{1,0:T(8,128)(2,1)} %constant.58.clone.across_ref, bf16[1024,256]{1,0:T(8,128)(2,1)} %constant.56.clone.back_ref, ...), custom_call_target="tpu_custom_call" | custom-call | tf_op jit(solution)/shard_map/mix_back/pallas_call | solution.py:238
  319.5 45.7 %from_owner.3.gathered_ref = f32[4,8,16,8,256]{4,3,2,1,0:T(8,128)} custom-call(f32[8,16,8,256]{3,2,1,0:T(8,128)} %bitcast.26), custom_call_target="tpu_custom_call" | custom-call | tf_op jit(solution)/shard_map/from_owner/pallas_call | solution.py:790
  365.3 18.4 %last_pass.1 = bf16[16,1024,512]{2,1,0:T(8,128)(2,1)} custom-call(f32[4,8,16,8,256]{4,3,2,1,0:T(8,128)} %from_owner.3.gathered_ref, bf16[16,1024,512]{2,1,0:T(8,128)(2,1)} %get-tuple-element.20.dpre_ref, bf16[1024,1024]{1,0:T(8,128)(2,1)} %get-tuple-element.31.up_ref, bf16[64,512]{1,0:T(8,128)(2,1)} %constant.64.clone.depth_ref.depth_low_ref, ...), custom_call_target="tpu_custom_call" | custom-call | tf_op jit(solution)/shard_map/last_pass/pallas_call | solution.py:428
  (4 shorter events, 0.0 us)

commit v2 on v1

--- a/solution.py
+++ b/solution.py
@@ -197,6 +197,12 @@
     return pl.BlockSpec(array.shape, lambda i: (0,) * array.ndim)
 
 
+def kept_spec(array):
+    return pl.BlockSpec(
+        array.shape, lambda i: (0,) * array.ndim, pipeline_mode=pl.Buffered(1)
+    )
+
+
 def mix_modes(planes, weight, across, across_rest, back, back_rest, pick_c, sum_d):
     kept_rows, lanes = across.shape[0], planes.shape[1]
     steps, _, pairs = weight.shape
@@ -309,12 +315,25 @@
     bypass_ref,
     bias_ref,
     dpre_ref,
-    modes_ref,
-    weight_ref,
-    sums_ref,
+    planes_ref,
+    small_ref,
     turned,
     preact,
     swept,
+    weight_ref,
+    sums_ref,
+    modes_ref,
+    landed,
+    mate_in,
+    across_out,
+    across_in,
+    peer_out,
+    small,
+    peers_in,
+    pair_sums,
+    small_peer_sem,
+    small_pair_sem,
+    *sems,
 ):
     step = pl.program_id(0)
     rows, cells, depth_cells = source_ref.shape
@@ -323,8 +342,13 @@
     block = bypass_ref.shape[0]
     columns = cells // channels
 
+    chunks, start_sums, pair_sum, side_sum, finish = to_owner_steps(
+        modes_ref, landed, mate_in, across_out, across_in, peer_out, sems
+    )
+
     @pl.when(step == 0)
     def _():
+        greet(*neighbours())
         weight_ref[...] = jnp.zeros_like(weight_ref)
         sums_ref[...] = jnp.zeros_like(sums_ref)
 
@@ -343,7 +367,7 @@
             dpre_ref[row, window, :] = value.astype(low)
             return carry
 
-        lax.fori_loop(0, columns, one_column, 0)
+        lax.fori_loop(0, columns, one_column, 0, unroll=4)
         depth_sums = dot_rows(depth_low_ref[...], dpre_ref[row])
         sums_ref[...] += depth_sums[:8, :]
         swept[row * modes : (row + 1) * modes, :] = depth_sums.astype(low)
@@ -353,9 +377,76 @@
             total += dot_rows(source_ref[row, window, :], dpre_ref[row, window, :])
         weight_ref[...] = total
     for part in range(modes_ref.shape[0]):
-        modes_ref[part] = dot(
+        modes_ref[part, pl.ds(step * rows, rows)] = dot(
             swept[...], down_ref[:, part * lanes : (part + 1) * lanes]
         ).reshape(rows, modes, lanes)
+    for chunk in range(chunks):
+
+        @pl.when(step == chunk)
+        def _(chunk=chunk):
+            start_sums(chunk)
+            if chunk >= 1:
+                pair_sum(chunk - 1)
+            if chunk >= 2:
+                side_sum(chunk - 2)
+
+    @pl.when(step == chunks - 1)
+    def _():
+        row, column, mate, across = neighbours()
+        row_devices = peers_in.shape[0]
+
+        def peer_copy(offset):
+            peer = lax.rem(row + offset, row_devices)
+            return send(
+                small, peers_in.at[row], small_peer_sem, (offset - 1,), (peer, column)
+            )
+
+        def pair_copy(which, target):
+            return send(
+                pair_sums.at[2 * which],
+                pair_sums.at[2 * which + 1],
+                small_pair_sem,
+                (which,),
+                (row, target),
+            )
+
+        small[...] = jnp.zeros_like(small)
+        total = weight_ref[:channels, :channels]
+        for at in range(channels, block, channels):
+            total += weight_ref[at : at + channels, at : at + channels]
+        small[:channels, :channels] = total
+        total = sums_ref[:, :channels]
+        for at in range(channels, cells, channels):
+            total += sums_ref[:, at : at + channels]
+        small[channels:, :channels] = total
+        peers_in[row] = small[...]
+
+        def start_peer(offset, carry):
+            peer_copy(offset).start()
+            return carry
+
+        def wait_peer(offset, carry):
+            peer_copy(offset).wait()
+            return carry
+
+        lax.fori_loop(1, row_devices, start_peer, 0)
+        pair_sum(chunks - 1)
+        if chunks >= 2:
+            side_sum(chunks - 2)
+        lax.fori_loop(1, row_devices, wait_peer, 0)
+        total = peers_in[0]
+        for peer in range(1, row_devices):
+            total += peers_in[peer]
+        pair_sums[0] = total
+        pair_copy(0, mate).start()
+        side_sum(chunks - 1)
+        pair_copy(0, mate).wait()
+        pair_sums[2] = pair_sums[0] + pair_sums[1]
+        pair_copy(1, across).start()
+        finish()
+        planes_ref[...] = landed[...]
+        pair_copy(1, across).wait()
+        small_ref[...] = pair_sums[2] + pair_sums[3]
 
 
 def middle_pass(
@@ -368,7 +459,9 @@
     block = bypass.shape[0]
     step = min(4, slab_rows)
     row_spec = pl.BlockSpec((step, cells, depth_cells), lambda i: (i, 0, 0))
-    part_spec = pl.BlockSpec((parts, step, modes, lanes), lambda i: (0, i, 0, 0))
+    partial = jax.ShapeDtypeStruct((parts, slab_rows, modes, lanes), wide)
+    planes, buffers, sems = owner_scratch(partial, devices, slab_rows // step)
+    small = (channels + 8, 128)
     return pl.pallas_call(
         functools.partial(middle_kernel, channels),
         grid=(slab_rows // step,),
@@ -376,32 +469,43 @@
             pl.BlockSpec((parts, devices, step, owned, lanes), lambda i: (0, 0, i, 0, 0)),
             row_spec,
             row_spec,
-            whole_spec(up),
-            whole_spec(up_rest),
-            whole_spec(depth),
-            whole_spec(depth_low),
-            whole_spec(down),
-            whole_spec(bypass),
-            whole_spec(bias),
+            kept_spec(up),
+            kept_spec(up_rest),
+            kept_spec(depth),
+            kept_spec(depth_low),
+            kept_spec(down),
+            kept_spec(bypass),
+            kept_spec(bias),
         ],
         out_specs=[
             row_spec,
-            part_spec,
-            pl.BlockSpec((block, block), lambda i: (0, 0)),
-            pl.BlockSpec((8, cells), lambda i: (0, 0)),
+            pl.BlockSpec(planes.shape, lambda i: (0, 0, 0, 0)),
+            pl.BlockSpec(small, lambda i: (0, 0)),
         ],
         out_shape=[
             jax.ShapeDtypeStruct(source.shape, low),
-            jax.ShapeDtypeStruct((parts, slab_rows, modes, lanes), wide),
-            jax.ShapeDtypeStruct((block, block), wide),
-            jax.ShapeDtypeStruct((8, cells), wide),
+            planes,
+            jax.ShapeDtypeStruct(small, wide),
         ],
         scratch_shapes=[
             pltpu.VMEM((step, cells, 3 * modes), low),
             pltpu.VMEM((cells, depth_cells), wide),
             pltpu.VMEM((step * modes, cells), low),
-        ],
-        compiler_params=pltpu.CompilerParams(vmem_limit_bytes=VMEM_LIMIT),
+            pltpu.VMEM((block, block), wide),
+            pltpu.VMEM((8, cells), wide),
+            pltpu.VMEM(partial.shape, wide),
+            pltpu.VMEM(planes.shape, wide),
+            *buffers,
+            pltpu.VMEM(small, wide),
+            pltpu.VMEM((devices, *small), wide),
+            pltpu.VMEM((4, *small), wide),
+            pltpu.SemaphoreType.DMA((2, devices - 1)),
+            pltpu.SemaphoreType.DMA((2, 2)),
+            *sems,
+        ],
+        compiler_params=pltpu.CompilerParams(
+            collective_id=0, has_side_effects=True, vmem_limit_bytes=VMEM_LIMIT
+        ),
         name="middle_pass",
     )(gathered, source, cotangent, up, up_rest, depth, depth_low, down, bypass, bias)
 
@@ -564,20 +668,6 @@
                 mate_copy(chunk, half).wait_send()
 
     return chunks, start, pair_sum, side_sum, finish
-
-
-def to_owner_kernel(partial_ref, out_ref, mate_in, across_out, across_in, peer_out, *sems):
-    greet(*neighbours())
-    chunks, start, pair_sum, side_sum, finish = to_owner_steps(
-        partial_ref, out_ref, mate_in, across_out, across_in, peer_out, sems
-    )
-    for chunk in range(chunks):
-        start(chunk)
-    for chunk in range(chunks):
-        pair_sum(chunk)
-    for chunk in range(chunks):
-        side_sum(chunk)
-    finish()
 
 
 def masking_kernel(
@@ -647,7 +737,7 @@
             ).astype(low)
             return carry
 
-        lax.fori_loop(0, columns, one_column, 0)
+        lax.fori_loop(0, columns, one_column, 0, unroll=4)
         put(row).start()
         for step, chunk in plan[row]:
             step(chunk)
@@ -656,10 +746,9 @@
     finish()
 
 
-def owner_scratch(partial, row_devices):
+def owner_scratch(partial, row_devices, chunks):
     parts, slab_rows, modes, lanes = partial.shape
     owned = modes // row_devices
-    chunks = min(4, slab_rows)
     return jax.ShapeDtypeStruct((row_devices, slab_rows, owned, lanes), wide), [
         pltpu.VMEM((2, slab_rows, modes, lanes), wide),
         pltpu.VMEM((slab_rows, modes, lanes), wide),
@@ -675,24 +764,8 @@
 vmem_spec = pl.BlockSpec(memory_space=pltpu.VMEM)
 
 
-def to_owner(partial):
-    shape, buffers, sems = owner_scratch(partial, lax.axis_size("gx"))
-    planes = pl.pallas_call(
-        to_owner_kernel,
-        in_specs=[vmem_spec],
-        out_specs=vmem_spec,
-        out_shape=shape,
-        scratch_shapes=buffers + sems,
-        compiler_params=pltpu.CompilerParams(
-            collective_id=0, has_side_effects=True, vmem_limit_bytes=VMEM_LIMIT
-        ),
-        name="to_owner",
-    )(partial)
-    return planes.reshape(-1, planes.shape[3])
-
-
 def to_owner_masking(partial, cotangent, hash_key, channels, all_columns):
-    shape, buffers, sems = owner_scratch(partial, lax.axis_size("gx"))
+    shape, buffers, sems = owner_scratch(partial, lax.axis_size("gx"), min(4, partial.shape[1]))
     _, cells, depth_cells = cotangent.shape
     planes, masked = pl.pallas_call(
         functools.partial(masking_kernel, all_columns, channels),
@@ -861,7 +934,7 @@
     input_modes, spread = mix_modes(
         planes, weight, across_wide, across_rest, back_wide, back_rest, pick_c, sum_d
     )
-    dpre, partial, weight_local, sums_local = middle_pass(
+    dpre, back_planes, small = middle_pass(
         from_owner(spread, owned_modes),
         source,
         masked,
@@ -873,16 +946,18 @@
         bypass_in,
         channel_bias[:, None],
     )
-    weight_local = jnp.einsum(
-        "acad->cd", weight_local.reshape(group, channels, group, channels)
-    )
-    bias_local = jnp.sum(sums_local[0].reshape(slab_columns, channels), axis=0) / depth_low[
-        0, 0
-    ].astype(wide)
-    weight_total, bias_total = lax.psum((weight_local, bias_local), ("gx", "gy"))
+    weight_total = small[:channels, :channels]
+    bias_total = small[channels, :channels] / depth_low[0, 0].astype(wide)
     norm_scale = 1.0 / math.sqrt(all_rows * all_columns * depth_cells)
     grad_spectral, spread_back = mix_back(
-        to_owner(partial), input_modes, weight, across_wide, back_wide, pick_c, pick_d, sum_c
+        back_planes.reshape(planes.shape),
+        input_modes,
+        weight,
+        across_wide,
+        back_wide,
+        pick_c,
+        pick_d,
+        sum_c,
     )
     grad_input = last_pass(
         from_owner(spread_back, owned_modes), dpre, up_wide, depth_low, bypass_out

time: 384 us -> 298 us (0.78)
  Pallas kernels: 325 us -> 280 us
  blocking collectives: 40 us -> 0 us
    psum x1 -> x0, blocking collectives: 40 us -> none  [local(): lax.psum((weight_local, bias_local), ('gx', 'gy'))]
    pallas_call x1 -> x0, Pallas kernels: 38.2 us -> none  [to_owner(): pl.pallas_call(to_owner_kernel, in_specs=[vmem_spec], out_specs=vmem_spec...]
    pallas_call x1, Pallas kernels: 95.8 us -> 91.9 us  [middle_pass(): pl.pallas_call(functools.partial(middle_kernel, channels), grid=(slab_row...]
where the time goes in v2:
time: 298 us
  Pallas kernels  280 us (94%)
  local copies, waits for them, and re-layouts  13.5 us (5%)
  other arithmetic  3.36 us (1%)
    pallas_call x1, Pallas kernels, middle_pass(): pl.pallas_call(functools.partial(middle_kernel, channels), grid=(slab_row...  91.9 us
    pallas_call x2, Pallas kernels, from_owner(): pl.pallas_call(from_owner_kernel, in_specs=[vmem_spec], out_specs=vmem_sp...  86.6 us
    pallas_call x1, Pallas kernels, to_owner_masking(): pl.pallas_call(functools.partial(masking_kernel, all_columns, channels),...  43.6 us
    pallas_call x1, Pallas kernels, last_pass(): pl.pallas_call(last_kernel, grid=(slab_rows // step,), in_specs=[pl.Block...  18.4 us
    pallas_call x1, Pallas kernels, forward_local(): pl.pallas_call(forward_kernel, grid=(slab_rows // step,), in_specs=[pl.Bl...  16.7 us
    pallas_call x1, Pallas kernels, mix_modes(): pl.pallas_call(mix_kernel, grid=(steps,), in_specs=[whole_spec(planes), p...  11.7 us
    pallas_call x1, Pallas kernels, mix_back(): pl.pallas_call(mix_back_kernel, grid=(steps,), in_specs=[whole_spec(plane...  11.3 us

profile of v2, /device:TPU:13, one launch (start us, length us, event | category | flops | bytes accessed | tf_op | source)
XLA Modules:
  0.0 297.6 jit_solution(138158325567482160)
XLA Ops:
  0.6 0.8 copy.24
  1.4 1.3 copy.25.bias_ref
  2.8 0.8 broadcast_multiply_fusion
  3.6 1.0 mul.68.bypass_ref
  4.6 1.0 mul.65.bypass_ref
  5.6 4.7 %constant_dynamic-slice_fusion = (bf16[1024,1024]{1,0:T(8,128)(2,1)}, bf16[1024,1024]{1,0:T(8,128)(2,1)}) fusion(bf16[4096,1024]{1,0:T(8,128)(2,1)} %constant.50.clone, s32[]{:T(128)S(6)} %select_n.9, bf16[4096,1024]{1,0:T(8,128)(2,1)} %constant.49.clone), kind=kLoop, calls=%fused_computation.7 | loop fusion | bytes 8388612 | tf_op jit(solution)/shard_map/dynamic_slice | solution.py:900
  10.3 16.7 %forward_local.1.partial_ref = f32[4,16,64,256]{3,2,1,0:T(8,128)} custom-call(bf16[16,1024,512]{2,1,0:T(8,128)(2,1)} %bitcast.21, bf16[64,512]{1,0:T(8,128)(2,1)} %constant.61.clone.depth_ref.depth_low_ref, bf16[1024,1024]{1,0:T(8,128)(2,1)} %get-tuple-element.25.down_ref, bf16[1024,1024]{1,0:T(8,128)(2,1)} %get-tuple-element.24.rest_ref), custom_call_target="tpu_custom_call" | custom-call | tf_op jit(solution)/shard_map/forward_local/pallas_call | solution.py:107
  27.0 4.7 %dynamic-slice_bitcast_fusion = (bf16[1024,1024]{1,0:T(8,128)(2,1)}, bf16[1024,1024]{1,0:T(8,128)(2,1)}) fusion(bf16[4,1024,1024]{2,1,0:T(8,128)(2,1)} %constant.52.clone, s32[]{:T(128)S(6)} %select_n.10, bf16[4,1024,1024]{2,1,0:T(8,128)(2,1)} %constant.51.clone), kind=kLoop, calls=%fused_computation | loop fusion | bytes 8388612 | tf_op jit(solution)/shard_map/jit(dynamic_index_in_dim)/squeeze | solution.py:903
  31.7 43.6 %to_owner_masking.1 = (f32[8,16,8,256]{3,2,1,0:T(8,128)}, bf16[16,1024,512]{2,1,0:T(8,128)(2,1)}) custom-call(s32[2]{0:T(128)} %key_ref.1, f32[4,16,64,256]{3,2,1,0:T(8,128)} %forward_local.1.partial_ref, bf16[16,1024,512]{2,1,0:T(8,128)(2,1)} %bitcast.24), custom_call_target="tpu_custom_call" | custom-call | tf_op jit(solution)/shard_map/to_owner_masking/pallas_call | solution.py:770
  75.3 11.7 %mix_modes.1 = (f32[256,256]{1,0:T(8,128)}, f32[1024,256]{1,0:T(8,128)}) custom-call(f32[1024,256]{1,0:T(8,128)} %bitcast.30, bf16[8,256,1024]{2,1,0:T(8,128)(2,1)} %bitcast.25, bf16[256,1024]{1,0:T(8,128)(2,1)} %constant.55.clone.across_ref, bf16[256,1024]{1,0:T(8,128)(2,1)} %constant.56.clone.across_rest, bf16[1024,256]{1,0:T(8,128)(2,1)} %constant.53.clone.back_ref, ...), custom_call_target="tpu_custom_call" | custom-call | tf_op jit(solution)/shard_map/mix_modes/pallas_call | solution.py:210
  86.9 42.9 %from_owner.2.gathered_ref = f32[4,8,16,8,256]{4,3,2,1,0:T(8,128)} custom-call(f32[8,16,8,256]{3,2,1,0:T(8,128)} %bitcast.28), custom_call_target="tpu_custom_call" | custom-call | tf_op jit(solution)/shard_map/from_owner/pallas_call | solution.py:863
  129.8 91.9 %middle_pass.1 = (bf16[16,1024,512]{2,1,0:T(8,128)(2,1)}, f32[8,16,8,256]{3,2,1,0:T(8,128)}, f32[40,128]{1,0:T(8,128)}) custom-call(f32[4,8,16,8,256]{4,3,2,1,0:T(8,128)} %from_owner.2.gathered_ref, bf16[16,1024,512]{2,1,0:T(8,128)(2,1)} %bitcast.22, bf16[16,1024,512]{2,1,0:T(8,128)(2,1)} %get-tuple-element.15.cotangent_ref, ...), custom_call_target="tpu_custom_call" | custom-call | tf_op jit(solution)/shard_map/middle_pass/pallas_call | solution.py:465
  221.7 1.2 multiply_bitcast_fusion
  222.9 1.3 slice_multiply_fusion
  224.2 11.3 %mix_back.1 = (f32[8,256,1024]{2,1,0:T(8,128)}, f32[1024,256]{1,0:T(8,128)}) custom-call(f32[1024,256]{1,0:T(8,128)} %bitcast.29, f32[256,256]{1,0:T(8,128)} %get-tuple-element.17.modes_ref, bf16[8,256,1024]{2,1,0:T(8,128)(2,1)} %bitcast.26, bf16[256,1024]{1,0:T(8,128)(2,1)} %constant.55.clone.across_ref, bf16[1024,256]{1,0:T(8,128)(2,1)} %constant.53.clone.back_ref, ...), custom_call_target="tpu_custom_call" | custom-call | tf_op jit(solution)/shard_map/mix_back/pallas_call | solution.py:244
  235.6 43.7 %from_owner.3.gathered_ref = f32[4,8,16,8,256]{4,3,2,1,0:T(8,128)} custom-call(f32[8,16,8,256]{3,2,1,0:T(8,128)} %bitcast.27), custom_call_target="tpu_custom_call" | custom-call | tf_op jit(solution)/shard_map/from_owner/pallas_call | solution.py:863
  279.3 18.4 %last_pass.1 = bf16[16,1024,512]{2,1,0:T(8,128)(2,1)} custom-call(f32[4,8,16,8,256]{4,3,2,1,0:T(8,128)} %from_owner.3.gathered_ref, bf16[16,1024,512]{2,1,0:T(8,128)(2,1)} %get-tuple-element.19.dpre_ref, bf16[1024,1024]{1,0:T(8,128)(2,1)} %get-tuple-element.27.up_ref, bf16[64,512]{1,0:T(8,128)(2,1)} %constant.61.clone.depth_ref.depth_low_ref, ...), custom_call_target="tpu_custom_call" | custom-call | tf_op jit(solution)/shard_map/last_pass/pallas_call | solution.py:532
  (1 shorter events, 0.0 us)
